TPU v7x, 32 devices: a whole 2x2x4 slice. The times are simulated.
32 devices in a mesh: fsdp: 4 (over y, x), ctx: 8 (over z, core).
Axes of the slice: x: 2, y: 2, z: 4, core: 2. Of those that a mesh axis runs over, the one named last changes fastest.
Arguments:
- inputs: bfloat16 [4, 1024, 2048], P('fsdp', 'ctx'), may hold values from -6 to 6
- queries: bfloat16 [4, 1024, 3072], P('fsdp', 'ctx'), may hold values from -210 to 210
- kv_down: bfloat16 [2048, 576], replicated, may hold values from -0.125 to 0.125
- latent_gain: bfloat16 [512], replicated, may hold values from 0.25 to 1.75
- kv_up: bfloat16 [512, 4096], replicated, may hold values from -0.25 to 0.25
- out_proj: bfloat16 [2048, 2048], replicated, may hold values from -0.125 to 0.125
- post_gain: bfloat16 [2048], replicated, may hold values from 0.25 to 1.75
- expert_ids: int32 [4, 1024, 6], P('fsdp', 'ctx'), may hold values from 0 to 15, all different within a row; in each aligned block of 128 rows (0 to 127, 128 to 255, ..., all dimensions but the last counted through in order) at most 96 rows name the same one
- gates: float32 [4, 1024, 6], P('fsdp', 'ctx'), may hold values from 0.1 to 1
- gate_up: bfloat16 [16, 2048, 1536], P('ctx', 'fsdp'), may hold values from -0.125 to 0.125
- down_proj: bfloat16 [16, 2048, 768], P('ctx', 'fsdp'), may hold values from -0.21875 to 0.21875
Outputs:
- attn_out: bfloat16 [4, 1024, 2048], P('fsdp', 'ctx')
- moe_out: bfloat16 [4, 1024, 2048], P('fsdp', 'ctx')
Inputs may be any that keep to these rules, and one draw needn't show every extreme that they name: `expert_ids`: within the 128 consecutive positions of a sequence on one index of ctx, no expert is chosen by more than 96 picks, a bound that some block reaches. The 6 experts of a token differ.
All inputs are finite; a program needn't handle non-finite values.
Results may differ from a plain program's by a relative error of at most 0.02.
The roundings to bfloat16 on the way count: a program that leaves them out, or rounds other values in their place, can miss the bound.
Values may be sent and summed in bfloat16 or wider, within the bound.
No kernel may reach another device: no remote copies, remote signals or barrier semaphores. Data moves between devices by JAX's collectives and lax.ppermute only.
A program may use at most 192 MiB of HBM per device.

v0:
```python
import math
import jax
import jax.numpy as jnp
from jax import lax
from jax.sharding import PartitionSpec as P

HEADS = 16
NOPE = 128
ROPE = 64
VDIM = 128
EPSILON = 1e-06
NEG_LARGE = -1e30


def normalize(values, gain):
    mean_sq = jnp.mean(values * values, axis=-1, keepdims=True)
    return values * lax.rsqrt(mean_sq + EPSILON) * gain.astype(jnp.float32)


def rotate(values, angles):
    half = values.shape[-1] // 2
    first = values[..., :half]
    second = values[..., half:]
    cosine = jnp.cos(angles)
    sine = jnp.sin(angles)
    return jnp.concatenate(
        [first * cosine - second * sine, second * cosine + first * sine], axis=-1
    )


def angles_of(positions, width):
    half = width // 2
    freqs = jnp.exp(-(2.0 * jnp.arange(half, dtype=jnp.float32) / width) * math.log(10000.0))
    return positions.astype(jnp.float32)[:, None] * freqs[None, :]


def attend(state, query_rows, row_pos, piece, start, latent_width):

    def update(inner):
        peak_old, total_old, acc_old = inner
        scores = jnp.dot(query_rows, jnp.transpose(piece), preferred_element_type=jnp.float32)
        key_pos = jnp.arange(piece.shape[0], dtype=jnp.int32)
        allowed = key_pos[None, :] <= row_pos[:, None]
        scores = jnp.where(allowed, scores, NEG_LARGE)
        peak_new = jnp.maximum(peak_old, jnp.max(scores, axis=1))
        expo = jnp.where(allowed, jnp.exp(scores - peak_new[:, None]), 0.0)
        total_new = jnp.sum(expo, axis=1)
        values = piece[:, :latent_width]
        acc_new = jnp.dot(expo.astype(jnp.bfloat16), values, preferred_element_type=jnp.float32)
        return (peak_new, total_new, acc_new)

    def keep(inner):
        return inner

    return lax.cond(start <= jnp.max(row_pos), update, keep, state)


def per_device(
    inputs,
    queries,
    kv_down,
    latent_gain,
    kv_up,
    out_proj,
    post_gain,
    expert_ids,
    gates,
    gate_up,
    down_proj,
):
    tokens = inputs[0]
    rows = tokens.shape[0]
    width_model = tokens.shape[1]
    ctx_size = lax.axis_size("ctx")
    rank = lax.axis_index("ctx")
    positions = rank * rows + jnp.arange(rows, dtype=jnp.int32)
    angles = angles_of(positions, ROPE)
    latent_width = latent_gain.shape[0]
    compressed = jnp.dot(tokens, kv_down, preferred_element_type=jnp.float32)
    latent = normalize(compressed[:, :latent_width], latent_gain)
    key_rope = rotate(compressed[:, latent_width:], angles)
    cache = jnp.concatenate([latent, key_rope], axis=1).astype(jnp.bfloat16)
    up_heads = kv_up.reshape(latent_width, HEADS, NOPE + VDIM)
    scale = (NOPE + ROPE) ** (-0.5)
    half = rows // 2
    query_heads = queries[0].reshape(rows, HEADS, NOPE + ROPE)
    lower_query = query_heads[:half]
    upper_query = query_heads[half:]
    lower_pos = positions[:half]
    upper_pos = positions[half:]

    def pack_rows(query_part, query_pos):
        part_angles = angles_of(query_pos, ROPE)
        absorbed = jnp.einsum(
            "thn,lhn->thl",
            query_part[:, :, :NOPE],
            up_heads[:, :, :NOPE],
            preferred_element_type=jnp.float32,
        )
        query_rope = rotate(query_part[:, :, NOPE:].astype(jnp.float32), part_angles[:, None, :])
        packed_part = (jnp.concatenate([absorbed, query_rope], axis=2) * scale).astype(jnp.bfloat16)
        return packed_part.reshape(half * HEADS, packed_part.shape[2])

    lower_rows = pack_rows(lower_query, lower_pos)
    upper_rows = pack_rows(upper_query, upper_pos)
    lower_row_pos = jnp.repeat(lower_pos, HEADS)
    upper_row_pos = jnp.repeat(upper_pos, HEADS)

    def start_state():
        return (
            jnp.full((half * HEADS,), NEG_LARGE, jnp.float32),
            jnp.zeros((half * HEADS,), jnp.float32),
            jnp.zeros((half * HEADS, latent_width), jnp.float32),
        )

    piece = lax.all_gather(cache, "ctx", axis=0, tiled=True)
    start = jnp.int32(0)
    first = attend(start_state(), lower_rows, lower_row_pos, piece, start, latent_width)
    second = attend(start_state(), upper_rows, upper_row_pos, piece, start, latent_width)

    def head_rows(state):
        context_part = (
            (state[2] / state[1][:, None]).astype(jnp.bfloat16).reshape(half, HEADS, latent_width)
        )
        heads_part = jnp.einsum(
            "thl,lhv->thv", context_part, up_heads[:, :, NOPE:], preferred_element_type=jnp.float32
        )
        return heads_part.astype(jnp.bfloat16).reshape(half, HEADS * VDIM)

    lower_heads = head_rows(first)
    upper_heads = head_rows(second)
    heads = jnp.concatenate([lower_heads, upper_heads], axis=0)
    attn = jnp.dot(heads, out_proj, preferred_element_type=jnp.float32)
    attn_out = attn.astype(jnp.bfloat16)
    routed_in = normalize(tokens.astype(jnp.float32) + attn, post_gain).astype(jnp.bfloat16)
    local_experts = gate_up.shape[0]
    experts = local_experts * ctx_size
    top_count = expert_ids.shape[2]
    capacity = 2 * rows * top_count // experts
    picks = expert_ids[0].reshape(rows * top_count)
    onehot = (picks[:, None] == jnp.arange(experts, dtype=jnp.int32)[None, :]).astype(jnp.int32)
    before = jnp.cumsum(onehot, axis=0) - onehot
    slot = jnp.sum(before * onehot, axis=1)
    target = picks * capacity + slot
    owner = jnp.arange(rows * top_count, dtype=jnp.int32) // top_count
    outgoing = (
        jnp.zeros((experts * capacity, width_model), jnp.bfloat16).at[target].set(routed_in[owner])
    )
    arrived = lax.all_to_all(
        outgoing.reshape(experts, capacity, width_model),
        "ctx",
        split_axis=0,
        concat_axis=1,
        tiled=True,
    )
    hidden_width = down_proj.shape[2]
    full_gate_up, full_down = (
        lax.all_gather(gate_up, "fsdp", axis=1, tiled=True),
        lax.all_gather(down_proj, "fsdp", axis=1, tiled=True),
    )
    joint = jnp.einsum("erd,edf->erf", arrived, full_gate_up, preferred_element_type=jnp.float32)
    hidden = (jax.nn.silu(joint[..., :hidden_width]) * joint[..., hidden_width:]).astype(
        jnp.bfloat16
    )
    results = jnp.einsum("erf,edf->erd", hidden, full_down, preferred_element_type=jnp.float32)
    returned = lax.all_to_all(
        results.astype(jnp.bfloat16), "ctx", split_axis=1, concat_axis=0, tiled=True
    )
    picked = returned.reshape(experts * capacity, width_model)[target]
    weighted = picked.astype(jnp.float32) * gates[0].reshape(rows * top_count)[:, None]
    moe = jnp.sum(weighted.reshape(rows, top_count, width_model), axis=1).astype(jnp.bfloat16)
    return (attn_out[None], moe[None])


def solution(mesh):
    in_specs = (
        P("fsdp", "ctx", None),
        P("fsdp", "ctx", None),
        P(),
        P(),
        P(),
        P(),
        P(),
        P("fsdp", "ctx", None),
        P("fsdp", "ctx", None),
        P("ctx", "fsdp", None),
        P("ctx", "fsdp", None),
    )
    out_specs = (P("fsdp", "ctx", None), P("fsdp", "ctx", None))
    return jax.shard_map(
        per_device, mesh=mesh, in_specs=in_specs, out_specs=out_specs, check_vma=False
    )
```

profile of v0, /device:TPU:0, one launch (start us, length us, event | category | flops | bytes accessed | tf_op | source)
XLA Modules:
  0.0 487.7 jit_solution(18436922709212303032)
XLA Ops:
  7.3 1.6 copy-done
  8.8 1.8 fusion.66
  10.8 0.7 convert_element_type.110
  11.4 0.1 fusion.79
  11.6 0.1 multiply_convert_fusion.1
  11.7 0.7 pad_maximum_fusion
  12.5 0.7 all-gather.6.cloned.1.call-update
  13.3 0.1 eq.29
  13.4 0.1 eq.25
  13.6 0.8 fusion.87
  14.4 0.6 slice.83
  15.0 6.5 %copy.39 = bf16[512,4096]{0,1:T(8,128)(2,1)} copy(bf16[512,4096]{1,0:T(8,128)(2,1)} %param.19) | data formatting | bytes 8388608 | tf_op args[4]
  21.5 2.1 fusion.42
  23.6 1.2 copy.42
  24.9 0.7 broadcast_reduce_fusion.1
  26.2 1.6 slice.94
  27.9 2.1 fusion.45
  29.9 2.6 copy.48
  32.5 0.7 broadcast_reduce_fusion
  33.9 1.7 reduce-window.6
  35.6 0.3 slice_reduce_fusion
  35.9 0.1 copy.52
  36.0 0.1 mul.259
  36.2 0.6 pad_clamp_fusion.1
  36.9 0.6 fusion.82
  37.5 0.3 multiply_cosine_fusion.1
  37.9 0.2 multiply_subtract_fusion.1
  38.1 1.5 fusion.30
  39.7 0.2 multiply_subtract_fusion
  39.9 0.3 copy-done.2
  40.2 1.5 fusion.31
  41.7 13.9 %conditional.2 = (f32[1024]{0:T(1024)S(1)}, f32[1024,512]{1,0:T(8,128)S(1)}) conditional(s32[]{:T(128)} %convert_element_type.106, () %tuple.24, (s32[64,16]{1,0:T(8,128)S(1)}, bf16[1024,576]{1,0:T(8,128)(2,1)}, bf16[1024,576]{0,1:T(8,128)(2,1)}) %tuple.25), branch_computations={%region_2.0_spmd, %region_3.6_spmd} | conditional | flops 2295331840 | bytes 41988168 | solution.py:55
  42.0 5.7 %fusion.1 = (f32[1024]{0:T(1024)S(1)}, f32[1024,1024]{0,1:T(8,128)}) fusion(s32[1024]{0:T(1024)S(1)} %le.3, bf16[1024,576]{1,0:T(8,128)(2,1)} %get-tuple-element.13, bf16[1024,576]{0,1:T(8,128)(2,1)} %get-tuple-element.42), kind=kOutput, calls=%fused_computation.6 | convolution fusion | flops 1211104256 | bytes 6561792 | tf_op jit(solution)/shard_map/cond/branch_1_fun/dot_general | solution.py:41
  47.7 1.4 copy.43
  49.1 4.7 fusion.4
  53.9 0.5 copy-done.6
  54.4 1.2 fusion.3
  55.6 0.2 divide_convert_fusion.1
  55.8 2.5 fusion.54
  58.4 0.7 broadcast_in_dim.26
  59.1 13.2 %conditional.3 = (f32[1024]{0:T(1024)}, f32[1024,512]{1,0:T(8,128)S(1)}) conditional(s32[]{:T(128)} %convert_element_type.115, () %tuple.26, (s32[64,16]{1,0:T(8,128)}, bf16[1024,576]{1,0:T(8,128)(2,1)}, bf16[1024,576]{0,1:T(8,128)(2,1)S(1)}) %tuple.61), branch_computations={%region_7.8_spmd, %region_8.11_spmd} | conditional | flops 2295331840 | bytes 37269548 | solution.py:55
  59.1 0.8 le.22
  59.9 5.2 %fusion.14 = (f32[1024]{0:T(1024)S(1)}, f32[1024,1024]{0,1:T(8,128)}) fusion(s32[1024]{0:T(1024)S(1)} %le.22, bf16[1024,576]{1,0:T(8,128)(2,1)} %get-tuple-element.16, bf16[1024,576]{0,1:T(8,128)(2,1)S(1)} %get-tuple-element.45), kind=kOutput, calls=%fused_computation.21 | convolution fusion | flops 1211104256 | bytes 6561792 | tf_op jit(solution)/shard_map/cond/branch_1_fun/dot_general | solution.py:41
  65.1 1.4 copy.49
  66.6 3.9 fusion.17
  70.5 1.8 fusion.16
  72.3 1.0 divide_convert_fusion
  73.3 2.4 fusion.57
  75.8 4.8 multiply_reduce_fusion.1
  80.6 1.0 multiply_convert_fusion
  81.6 24.7 %scatter_custom_fusion = bf16[1536,2048]{1,0:T(8,128)(2,1)} fusion(s32[768]{0:T(1024)S(1)} %copy-done.9, bf16[128,2048]{1,0:T(8,128)(2,1)S(1)} %get-tuple-element.50, s32[1024]{0:T(1024)} %pad_clamp_fusion.1, bf16[]{:T(256)} %constant.32.clone.1), kind=kCustom, calls=%fused_computation.37 | custom fusion | bytes 6291968 | tf_op jit(solution)/shard_map/scatter | solution.py:147
  106.4 6.5 %all-to-all-start = ((bf16[16,96,2048]{2,1,0:T(8,128)(2,1)}), bf16[16,96,2048]{2,1,0:T(8,128)(2,1)}, u32[]{:S(2)}, u32[]{:S(2)}) async-start(bf16[16,96,2048]{2,1,0:T(8,128)(2,1)} %bitcast.75), calls=%async_computation | async-start | bytes 12582912 | tf_op jit(solution)/shard_map/all_to_all | solution.py:149
  112.9 0.7 all-gather.8.cloned.1.call-update
  113.6 138.3 %all-to-all-done = bf16[16,96,2048]{2,1,0:T(8,128)(2,1)} async-done(((bf16[16,96,2048]{2,1,0:T(8,128)(2,1)}), bf16[16,96,2048]{2,1,0:T(8,128)(2,1)}, u32[]{:S(2)}, u32[]{:S(2)}) %all-to-all-start) | async-done | bytes 6291488 | tf_op jit(solution)/shard_map/all_to_all | solution.py:149
  251.9 6.5 %copy.56 = bf16[2,8,96,2048]{3,2,1,0:T(8,128)(2,1)} copy(bf16[2,8,96,2048]{3,2,0,1:T(8,128)(2,1)} %bitcast.18) | data formatting | bytes 12582912 | tf_op jit(solution)/shard_map/all_to_all | solution.py:149
  258.5 17.0 %fusion.88 = f32[2,768,1536]{2,1,0:T(8,128)} fusion(bf16[2,768,2048]{2,1,0:T(8,128)(2,1)} %bitcast.82, bf16[2,2048,1536]{2,1,0:T(8,128)(2,1)} %all-gather.6.cloned.1.call-done), kind=kOutput, calls=%fused_computation.133 | convolution fusion | flops 9663676416 | bytes 28311552 | tf_op jit(solution)/shard_map/erd,edf->erf/dot_general | solution.py:161
  275.5 9.6 %convolution_convert_fusion = bf16[2,768,2048]{2,1,0:T(8,128)(2,1)S(1)} fusion(bf16[2,2048,768]{2,1,0:T(8,128)(2,1)} %all-gather.8.cloned.1.call-done, f32[2,768,1536]{2,1,0:T(8,128)} %fusion.88), kind=kOutput, calls=%fused_computation.36 | convolution fusion | flops 4842061824 | bytes 22020096 | tf_op jit(solution)/shard_map/erf,edf->erd/dot_general | solution.py:165
  285.0 18.8 %copy.57 = bf16[2,768,2048]{2,0,1:T(2,128)(2,1)} copy(bf16[2,768,2048]{2,1,0:T(8,128)(2,1)S(1)} %convolution_convert_fusion) | data formatting | bytes 12582912 | tf_op jit(solution)/shard_map/convert_element_type | solution.py:167
  303.8 5.0 %all-to-all-start.1 = ((bf16[2,768,2048]{2,0,1:T(2,128)(2,1)}), bf16[2,768,2048]{2,0,1:T(2,128)(2,1)}, u32[]{:S(2)}, u32[]{:S(2)}) async-start(bf16[2,768,2048]{2,0,1:T(2,128)(2,1)} %copy.57), calls=%async_computation.1 | async-start | bytes 12582912 | tf_op jit(solution)/shard_map/all_to_all | solution.py:166
  309.0 138.8 %all-to-all-done.1 = bf16[2,768,2048]{2,0,1:T(2,128)(2,1)} async-done(((bf16[2,768,2048]{2,0,1:T(2,128)(2,1)}), bf16[2,768,2048]{2,0,1:T(2,128)(2,1)}, u32[]{:S(2)}, u32[]{:S(2)}) %all-to-all-start.1) | async-done | bytes 6291488 | tf_op jit(solution)/shard_map/all_to_all | solution.py:166
  447.8 8.3 %copy.58 = bf16[2,8,96,2048]{3,2,0,1:T(8,128)(2,1)} copy(bf16[2,8,96,2048]{3,0,2,1:T(2,128)(2,1)} %bitcast.20) | data formatting | bytes 12582912 | tf_op jit(solution)/shard_map/all_to_all | solution.py:166
  456.1 10.7 %gather_fusion = bf16[768,2048]{1,0:T(8,128)(2,1)} fusion(bf16[1536,2048]{1,0:T(8,128)(2,1)} %bitcast.74, s32[1024]{0:T(1024)S(1)} %pad_clamp_fusion), kind=kCustom, calls=%fused_computation.1 | custom fusion | bytes 6294528 | tf_op jit(solution)/shard_map/gather | solution.py:169
  466.8 6.6 %reshape.286 = f32[128,6,2048]{2,1,0:T(8,128)} reshape(bf16[768,2048]{1,0:T(8,128)(2,1)} %gather_fusion) | data formatting | bytes 9437184 | tf_op jit(solution)/shard_map/convert_element_type | solution.py:170
  473.4 7.5 %multiply_reduce_fusion = bf16[128,2048]{1,0:T(8,128)(2,1)} fusion(f32[128,6,2048]{2,1,0:T(8,128)} %reshape.286, f32[128,6]{1,0:T(8,128)S(1)} %bitcast.92), kind=kLoop, calls=%fused_computation.33 | loop fusion | flops 2883584 | bytes 6818816 | tf_op jit(solution)/shard_map/reduce_sum | solution.py:171
  (55 shorter events, 1.2 us)
Async XLA Ops:
  7.2 1.7 copy-start
  7.2 6.0 %copy-start.10 = (s32[1,128,6]{1,0,2:T(1,128)S(1)}, s32[1,128,6]{1,0,2:T(1,128)}, u32[]{:S(2)}) copy-start(s32[1,128,6]{1,0,2:T(1,128)} %param.22) | copy-start | bytes 9220
  7.2 6.4 %copy-start.8 = (bf16[1,128,3072]{2,1,0:T(8,128)(2,1)S(1)}, bf16[1,128,3072]{2,1,0:T(8,128)(2,1)}, u32[]{:S(2)}) copy-start(bf16[1,128,3072]{2,1,0:T(8,128)(2,1)} %param.16) | copy-start | bytes 2359300
  7.2 34.5 %all-gather.4.cloned.1.call-start = ((), (), s32[]{:S(2)}) async-start(), calls=%async_computation.2 | async-start | bytes 1327104 | tf_op jit(solution)/shard_map/all_gather | solution.py:116
  12.4 246.1 %all-gather.6.cloned.1.call-start = ((), (), s32[]{:S(2)}) async-start(), calls=%async_computation.3 | async-start | bytes 15728640 | tf_op jit(solution)/shard_map/all_gather | solution.py:158
  27.9 6.0 %copy-start.11 = (bf16[2048]{0:T(1024)(128)(2,1)S(1)}, bf16[2048]{0:T(1024)(128)(2,1)}, u32[]{:S(2)}) copy-start(bf16[2048]{0:T(1024)(128)(2,1)} %param.21) | copy-start | bytes 12292
  38.1 2.1 copy-start.2
  42.0 5.7 %copy-start.5 = (bf16[1024,576]{0,1:T(8,128)(2,1)S(1)}, bf16[1024,576]{0,1:T(8,128)(2,1)}, u32[]{:S(2)}) copy-start(bf16[1024,576]{0,1:T(8,128)(2,1)} %get-tuple-element.42) | copy-start | bytes 3538948 | tf_op jit(solution)/shard_map/cond
  49.1 5.3 %copy-start.6 = (f32[1024,1024]{0,1:T(8,128)S(1)}, f32[1024,1024]{0,1:T(8,128)}, u32[]{:S(2)}) copy-start(f32[1024,1024]{0,1:T(8,128)} %get-tuple-element.47) | copy-start | bytes 12582916 | tf_op jit(solution)/shard_map/cond
  55.6 3.5 copy-start.4
  66.6 4.0 copy-start.7
  72.3 3.5 copy-start.3
  75.8 5.9 %copy-start.9 = (s32[768]{0:T(1024)S(1)}, s32[768]{0:T(1024)}, u32[]{:S(2)}) copy-start(s32[768]{0:T(1024)} %fusion.82) | copy-start | bytes 9220
  106.4 145.6 %all-to-all-start = ((bf16[16,96,2048]{2,1,0:T(8,128)(2,1)}), bf16[16,96,2048]{2,1,0:T(8,128)(2,1)}, u32[]{:S(2)}, u32[]{:S(2)}) async-start(bf16[16,96,2048]{2,1,0:T(8,128)(2,1)} %bitcast.75), calls=%async_computation | async-start | bytes 12582912 | tf_op jit(solution)/shard_map/all_to_all | solution.py:149
  112.9 162.6 %all-gather.8.cloned.1.call-start = ((), (), s32[]{:S(2)}) async-start(), calls=%async_computation.4 | async-start | bytes 7864320 | tf_op jit(solution)/shard_map/all_gather | solution.py:159
  303.8 5.1 %copy-start.12 = (f32[1,128,6]{1,0,2:T(1,128)S(1)}, f32[1,128,6]{1,0,2:T(1,128)}, u32[]{:S(2)}) copy-start(f32[1,128,6]{1,0,2:T(1,128)} %param.23) | copy-start | bytes 9220
  303.8 144.0 %all-to-all-start.1 = ((bf16[2,768,2048]{2,0,1:T(2,128)(2,1)}), bf16[2,768,2048]{2,0,1:T(2,128)(2,1)}, u32[]{:S(2)}, u32[]{:S(2)}) async-start(bf16[2,768,2048]{2,0,1:T(2,128)(2,1)} %copy.57), calls=%async_computation.1 | async-start | bytes 12582912 | tf_op jit(solution)/shard_map/all_to_all | solution.py:166
  473.4 7.5 %copy-start.1 = (bf16[2048,576]{0,1:T(8,128)(2,1)S(1)}, bf16[2048,576]{0,1:T(8,128)(2,1)}, u32[]{:S(2)}) copy-start(bf16[2048,576]{0,1:T(8,128)(2,1)} %param.17) | copy-start | bytes 7077892
Sparse Core Ops, SparseCore 0:
  12.5 27.4 all-gather.3
  41.9 121.3 all-gather.5
  165.1 70.1 all-gather.7
where the time goes:
time: 495 us; the launch traced here: 488 us
  waiting for transfers between devices  279 us (56%)
  local copies, waits for them, and re-layouts  97.1 us (20%)
  matrix products  61.8 us (12%)
  other arithmetic  22.9 us (5%)
  between operations  15.5 us (3%)
  starting transfers between devices  11.7 us (2%)
    all_to_all x1, waiting for transfers between devices, per_device(): lax.all_to_all(results.astype(jnp.bfloat16), 'ctx', split_axis=1, concat_...  139 us
    all_to_all x1, waiting for transfers between devices, per_device(): lax.all_to_all(outgoing.reshape(experts, capacity, width_model), 'ctx', s...  138 us
    scatter x1, local copies, waits for them, and re-layouts, per_device(): jnp.zeros((experts * capacity, width_model), jnp.bfloat16).at[target]  24.7 us
    convert_element_type x1, local copies, waits for them, and re-layouts, per_device(): results.astype(jnp.bfloat16)  18.8 us
    dot_general x1, matrix products, per_device(): jnp.einsum('erd,edf->erf', arrived, full_gate_up, preferred_element_type=...  17 us
    dot_general x2, matrix products, update(): jnp.dot(query_rows, jnp.transpose(piece), preferred_element_type=jnp.floa...  10.9 us
    gather x1, local copies, waits for them, and re-layouts, per_device(): picked = returned.reshape(experts * capacity, width_model)[target]  10.7 us
  transfers between devices with their start and end apart: 5, of which 2 were waited for; matrix products, arithmetic and copies ran while one was open for 23% of the time, Pallas kernels for 0%

commit v1 on v0

--- a/solution.py
+++ b/solution.py
@@ -10,6 +10,17 @@
 VDIM = 128
 EPSILON = 1e-06
 NEG_LARGE = -1e30
+
+
+def in_blocks(x, dim, count):
+    before, after = (x.shape[:dim], x.shape[dim + 1 :])
+    return jnp.moveaxis(x.reshape(*before, count, -1, *after), dim, 0)
+
+
+def laid_out(pieces, dim):
+    shape = list(pieces.shape[1:])
+    shape[dim] *= pieces.shape[0]
+    return jnp.moveaxis(pieces, 0, dim).reshape(shape)
 
 
 def normalize(values, gain):
@@ -163,9 +174,15 @@
         jnp.bfloat16
     )
     results = jnp.einsum("erf,edf->erd", hidden, full_down, preferred_element_type=jnp.float32)
-    returned = lax.all_to_all(
-        results.astype(jnp.bfloat16), "ctx", split_axis=1, concat_axis=0, tiled=True
-    )
+    shard = results.astype(jnp.bfloat16)
+    size, here = (lax.axis_size("ctx"), lax.axis_index("ctx"))
+    parts = in_blocks(shard, 1, size)
+    outs = [parts[here]]
+    for hop in range(1, size):
+        sent = parts[here ^ hop]
+        outs.append(lax.ppermute(sent, "ctx", [(i, i ^ hop) for i in range(size)]))
+    parts = jnp.stack(outs)[here ^ jnp.arange(size)]
+    returned = laid_out(parts, 0)
     picked = returned.reshape(experts * capacity, width_model)[target]
     weighted = picked.astype(jnp.float32) * gates[0].reshape(rows * top_count)[:, None]
     moe = jnp.sum(weighted.reshape(rows, top_count, width_model), axis=1).astype(jnp.bfloat16)

time: 495 us -> 473 us (0.956)
  the two profiles are of different devices: /device:TPU:0 before, /device:TPU:9 now
where the time goes in v1:
time: 473 us; the launch traced here: 466 us
  waiting for transfers between devices  259 us (55%)
  local copies, waits for them, and re-layouts  91 us (19%)
  matrix products  62.2 us (13%)
  other arithmetic  22.9 us (5%)
  between operations  15.7 us (3%)
  starting transfers between devices  14.9 us (3%)
    all_to_all x1, waiting for transfers between devices, per_device(): lax.all_to_all(outgoing.reshape(experts, capacity, width_model), 'ctx', s...  135 us
    ppermute x7, waiting for transfers between devices, per_device(): outs.append(lax.ppermute(sent, 'ctx', [(i, i ^ hop) for i in range(size)]))  123 us
    scatter x1, local copies, waits for them, and re-layouts, per_device(): jnp.zeros((experts * capacity, width_model), jnp.bfloat16).at[target]  24.7 us
    unnamed x31, local copies, waits for them, and re-layouts  19.9 us
    dot_general x1, matrix products, per_device(): jnp.einsum('erd,edf->erf', arrived, full_gate_up, preferred_element_type=...  16.9 us
    dot_general x2, matrix products, update(): jnp.dot(query_rows, jnp.transpose(piece), preferred_element_type=jnp.floa...  11.3 us
    gather x1, local copies, waits for them, and re-layouts, per_device(): picked = returned.reshape(experts * capacity, width_model)[target]  10.7 us
    dot_general x1, matrix products, per_device(): jnp.einsum('erf,edf->erd', hidden, full_down, preferred_element_type=jnp....  9.57 us
  transfers between devices with their start and end apart: 11, of which 6 were waited for; matrix products, arithmetic and copies ran while one was open for 27% of the time, Pallas kernels for 0%

profile of v1, /device:TPU:9, one launch (start us, length us, event | category | flops | bytes accessed | tf_op | source)
XLA Modules:
  0.0 465.8 jit_solution(9489844578272856406)
XLA Ops:
  7.3 1.6 copy-done
  8.8 1.8 fusion.66
  10.8 0.7 convert_element_type.110
  11.7 0.7 pad_maximum_fusion
  12.5 0.7 all-gather.6.cloned.1.call-update
  13.6 0.8 fusion.88
  15.0 6.5 %copy.18 = bf16[512,4096]{0,1:T(8,128)(2,1)} copy(bf16[512,4096]{1,0:T(8,128)(2,1)} %param.19) | data formatting | bytes 8388608 | tf_op args[4]
  21.6 2.1 fusion.42
  23.7 1.2 copy.21
  25.0 0.7 broadcast_reduce_fusion.1
  26.3 1.6 slice.94
  28.0 2.0 fusion.45
  30.1 2.6 copy.27
  32.6 0.7 broadcast_reduce_fusion
  34.0 1.7 reduce-window.6
  38.2 1.5 fusion.30
  40.2 1.5 fusion.31
  41.8 14.2 %conditional.2 = (f32[1024]{0:T(1024)S(1)}, f32[1024,512]{1,0:T(8,128)S(1)}) conditional(s32[]{:T(128)} %convert_element_type.106, () %tuple.24, (s32[64,16]{1,0:T(8,128)S(1)}, bf16[1024,576]{1,0:T(8,128)(2,1)}, bf16[1024,576]{0,1:T(8,128)(2,1)}) %tuple.25), branch_computations={%region_2.0_spmd, %region_3.6_spmd} | conditional | flops 2295331840 | bytes 41988168 | solution.py:66
  42.0 6.1 %fusion.1 = (f32[1024]{0:T(1024)S(1)}, f32[1024,1024]{0,1:T(8,128)}) fusion(s32[1024]{0:T(1024)S(1)} %le.3, bf16[1024,576]{1,0:T(8,128)(2,1)} %get-tuple-element.13, bf16[1024,576]{0,1:T(8,128)(2,1)} %get-tuple-element.36), kind=kOutput, calls=%fused_computation.7 | convolution fusion | flops 1211104256 | bytes 6561792 | tf_op jit(solution)/shard_map/cond/branch_1_fun/dot_general | solution.py:52
  48.2 1.4 copy.22
  49.6 4.7 %fusion.4 = f32[1024,512]{1,0:T(8,128)S(1)} fusion(f32[1024,1024]{0,1:T(8,128)} %get-tuple-element.41, f32[1024]{0:T(1024)S(1)} %broadcast_maximum_fusion, s32[1024]{0:T(1024)S(1)} %le.3, bf16[1024,576]{1,0:T(8,128)(2,1)} %copy.22), kind=kOutput, calls=%fused_computation.10 | convolution fusion | flops 1078984704 | bytes 7348224 | tf_op jit(solution)/shard_map/cond/branch_1_fun/dot_general | solution.py:60
  54.8 1.2 fusion.3
  56.2 2.5 fusion.54
  58.8 0.7 broadcast_in_dim.26
  59.5 13.2 %conditional.3 = (f32[1024]{0:T(1024)}, f32[1024,512]{1,0:T(8,128)S(1)}) conditional(s32[]{:T(128)} %convert_element_type.115, () %tuple.26, (s32[64,16]{1,0:T(8,128)}, bf16[1024,576]{1,0:T(8,128)(2,1)}, bf16[1024,576]{0,1:T(8,128)(2,1)S(1)}) %tuple.66), branch_computations={%region_7.8_spmd, %region_8.11_spmd} | conditional | flops 2295331840 | bytes 37269548 | solution.py:66
  59.5 0.8 le.22
  60.4 5.2 %fusion.14 = (f32[1024]{0:T(1024)S(1)}, f32[1024,1024]{0,1:T(8,128)}) fusion(s32[1024]{0:T(1024)S(1)} %le.22, bf16[1024,576]{1,0:T(8,128)(2,1)} %get-tuple-element.16, bf16[1024,576]{0,1:T(8,128)(2,1)S(1)} %get-tuple-element.39), kind=kOutput, calls=%fused_computation.22 | convolution fusion | flops 1211104256 | bytes 6561792 | tf_op jit(solution)/shard_map/cond/branch_1_fun/dot_general | solution.py:52
  65.6 1.4 copy.28
  67.0 4.0 fusion.17
  71.0 1.8 fusion.16
  72.8 1.0 divide_convert_fusion
  73.7 2.4 fusion.57
  76.2 4.8 %multiply_reduce_fusion.1 = (f32[128]{0:T(128)S(1)}, f32[128,2048]{1,0:T(8,128)S(1)}) fusion(bf16[1,128,2048]{2,1,0:T(8,128)(2,1)S(1)} %copy-done.4, bf16[2048,2048]{1,0:T(8,128)(2,1)} %param.20, bf16[64,2048]{1,0:T(8,128)(2,1)S(1)} %bitcast.120, bf16[64,2048]{1,0:T(8,128)(2,1)S(1)} %bitcast.119), kind=kOutput, calls=%fused_computation.65 | convolution fusion | flops 1075838848 | bytes 10486272 | tf_op jit(solution)/shard_map/dot_general | solution.py:144
  81.0 1.0 multiply_convert_fusion
  82.1 24.7 %scatter_custom_fusion = bf16[1536,2048]{1,0:T(8,128)(2,1)} fusion(s32[768]{0:T(1024)S(1)} %copy-done.10, bf16[128,2048]{1,0:T(8,128)(2,1)S(1)} %get-tuple-element.51, s32[1024]{0:T(1024)} %pad_clamp_fusion.2, bf16[]{:T(256)} %constant.22.clone.1), kind=kCustom, calls=%fused_computation.38 | custom fusion | bytes 6291968 | tf_op jit(solution)/shard_map/scatter | solution.py:158
  106.8 5.5 %all-to-all-start = ((bf16[16,96,2048]{2,1,0:T(8,128)(2,1)}), bf16[16,96,2048]{2,1,0:T(8,128)(2,1)}, u32[]{:S(2)}, u32[]{:S(2)}) async-start(bf16[16,96,2048]{2,1,0:T(8,128)(2,1)} %bitcast.105), calls=%async_computation | async-start | bytes 12582912 | tf_op jit(solution)/shard_map/all_to_all | solution.py:160
  112.2 0.7 all-gather.8.cloned.1.call-update
  113.0 134.6 %all-to-all-done = bf16[16,96,2048]{2,1,0:T(8,128)(2,1)} async-done(((bf16[16,96,2048]{2,1,0:T(8,128)(2,1)}), bf16[16,96,2048]{2,1,0:T(8,128)(2,1)}, u32[]{:S(2)}, u32[]{:S(2)}) %all-to-all-start) | async-done | bytes 6291488 | tf_op jit(solution)/shard_map/all_to_all | solution.py:160
  247.6 6.5 %copy.35 = bf16[2,8,96,2048]{3,2,1,0:T(8,128)(2,1)} copy(bf16[2,8,96,2048]{3,2,0,1:T(8,128)(2,1)} %bitcast.18) | data formatting | bytes 12582912 | tf_op jit(solution)/shard_map/all_to_all | solution.py:160
  254.2 16.9 %fusion.89 = f32[2,768,1536]{2,1,0:T(8,128)} fusion(bf16[2,768,2048]{2,1,0:T(8,128)(2,1)} %bitcast.114, bf16[2,2048,1536]{2,1,0:T(8,128)(2,1)} %all-gather.6.cloned.1.call-done), kind=kOutput, calls=%fused_computation.152 | convolution fusion | flops 9663676416 | bytes 28311552 | tf_op jit(solution)/shard_map/erd,edf->erf/dot_general | solution.py:172
  271.1 9.6 %convolution_convert_fusion = bf16[2,768,2048]{2,1,0:T(8,128)(2,1)S(1)} fusion(bf16[2,2048,768]{2,1,0:T(8,128)(2,1)} %all-gather.8.cloned.1.call-done, f32[2,768,1536]{2,1,0:T(8,128)} %fusion.89), kind=kOutput, calls=%fused_computation.37 | convolution fusion | flops 4842061824 | bytes 22020096 | tf_op jit(solution)/shard_map/erf,edf->erd/dot_general | solution.py:176
  280.7 2.2 dynamic-slice_bitcast_fusion
  282.9 1.1 copy-done.3
  284.5 3.4 collective-permute-start.1
  288.1 1.5 collective-permute-start.3
  289.5 1.5 collective-permute-start.4
  291.0 2.1 bitcast_dynamic-update-slice_fusion.7
  293.2 2.1 bitcast_dynamic-update-slice_fusion.6
  295.3 40.7 %collective-permute-done.1 = bf16[2,96,2048]{2,1,0:T(8,128)(2,1)} collective-permute-done((bf16[2,96,2048]{2,1,0:T(8,128)(2,1)}, bf16[2,96,2048]{2,1,0:T(8,128)(2,1)}, u32[]{:S(2)}, u32[]{:S(2)}) %collective-permute-start.1) | collective-permute-done | bytes 786464 | tf_op jit(solution)/shard_map/ppermute | solution.py:183
  335.9 2.5 collective-permute-start.6
  338.4 2.2 bitcast_dynamic-update-slice_fusion.5
  340.5 12.2 %collective-permute-done.2 = bf16[2,96,2048]{2,1,0:T(8,128)(2,1)S(1)} collective-permute-done((bf16[2,96,2048]{2,1,0:T(8,128)(2,1)}, bf16[2,96,2048]{2,1,0:T(8,128)(2,1)S(1)}, u32[]{:S(2)}, u32[]{:S(2)}) %collective-permute-start.2) | collective-permute-done | bytes 786464 | tf_op jit(solution)/shard_map/ppermute | solution.py:183
  352.8 1.1 bitcast_dynamic-update-slice_fusion.4
  353.8 1.0 bitcast_dynamic-update-slice_fusion.3
  354.8 35.9 %collective-permute-done.4 = bf16[2,96,2048]{2,1,0:T(8,128)(2,1)S(1)} collective-permute-done((bf16[2,96,2048]{2,1,0:T(8,128)(2,1)S(1)}, bf16[2,96,2048]{2,1,0:T(8,128)(2,1)S(1)}, u32[]{:S(2)}, u32[]{:S(2)}) %collective-permute-start.4) | collective-permute-done | bytes 786464 | tf_op jit(solution)/shard_map/ppermute | solution.py:183
  390.6 1.0 bitcast_dynamic-update-slice_fusion.2
  391.6 17.9 %collective-permute-done.5 = bf16[2,96,2048]{2,1,0:T(8,128)(2,1)S(1)} collective-permute-done((bf16[2,96,2048]{2,1,0:T(8,128)(2,1)S(1)}, bf16[2,96,2048]{2,1,0:T(8,128)(2,1)S(1)}, u32[]{:S(2)}, u32[]{:S(2)}) %collective-permute-start.5) | collective-permute-done | bytes 786464 | tf_op jit(solution)/shard_map/ppermute | solution.py:183
  409.5 1.0 bitcast_dynamic-update-slice_fusion.1
  410.5 16.2 %collective-permute-done.6 = bf16[2,96,2048]{2,1,0:T(8,128)(2,1)S(1)} collective-permute-done((bf16[2,96,2048]{2,1,0:T(8,128)(2,1)S(1)}, bf16[2,96,2048]{2,1,0:T(8,128)(2,1)S(1)}, u32[]{:S(2)}, u32[]{:S(2)}) %collective-permute-start.6) | collective-permute-done | bytes 786464 | tf_op jit(solution)/shard_map/ppermute | solution.py:183
  426.7 1.0 bitcast_dynamic-update-slice_fusion
  427.7 6.4 %gather_fusion = bf16[8,2,96,2048]{3,2,1,0:T(8,128)(2,1)} fusion(bf16[8,2,96,2048]{3,2,1,0:T(8,128)(2,1)} %bitcast_dynamic-update-slice_fusion, s32[1024]{0:T(1024)S(1)} %pad_clamp_fusion.1), kind=kCustom, calls=%fused_computation.1 | custom fusion | bytes 12582944 | tf_op jit(solution)/shard_map/gather | solution.py:184
  434.0 10.7 %gather_fusion.1 = bf16[768,2048]{1,0:T(8,128)(2,1)} fusion(bf16[1536,2048]{1,0:T(8,128)(2,1)} %bitcast.104, s32[1024]{0:T(1024)S(1)} %pad_clamp_fusion), kind=kCustom, calls=%fused_computation.2 | custom fusion | bytes 6294528 | tf_op jit(solution)/shard_map/gather | solution.py:186
  444.7 6.7 %reshape.316 = f32[128,6,2048]{2,1,0:T(8,128)} reshape(bf16[768,2048]{1,0:T(8,128)(2,1)} %gather_fusion.1) | data formatting | bytes 9437184 | tf_op jit(solution)/shard_map/convert_element_type | solution.py:187
  451.5 7.5 %multiply_reduce_fusion = bf16[128,2048]{1,0:T(8,128)(2,1)} fusion(f32[128,6,2048]{2,1,0:T(8,128)} %reshape.316, f32[128,6]{1,0:T(8,128)S(1)} %bitcast.124), kind=kLoop, calls=%fused_computation.34 | loop fusion | flops 2883584 | bytes 6818816 | tf_op jit(solution)/shard_map/reduce_sum | solution.py:188
  (78 shorter events, 6.3 us)
Async XLA Ops:
  7.2 1.7 copy-start
  7.2 6.0 %copy-start.11 = (s32[1,128,6]{1,0,2:T(1,128)S(1)}, s32[1,128,6]{1,0,2:T(1,128)}, u32[]{:S(2)}) copy-start(s32[1,128,6]{1,0,2:T(1,128)} %param.22) | copy-start | bytes 9220
  7.2 6.4 %copy-start.9 = (bf16[1,128,3072]{2,1,0:T(8,128)(2,1)S(1)}, bf16[1,128,3072]{2,1,0:T(8,128)(2,1)}, u32[]{:S(2)}) copy-start(bf16[1,128,3072]{2,1,0:T(8,128)(2,1)} %param.16) | copy-start | bytes 2359300
  7.2 34.5 %all-gather.4.cloned.1.call-start = ((), (), s32[]{:S(2)}) async-start(), calls=%async_computation.1 | async-start | bytes 1327104 | tf_op jit(solution)/shard_map/all_gather | solution.py:127
  12.4 241.7 %all-gather.6.cloned.1.call-start = ((), (), s32[]{:S(2)}) async-start(), calls=%async_computation.2 | async-start | bytes 15728640 | tf_op jit(solution)/shard_map/all_gather | solution.py:169
  28.0 6.0 %copy-start.12 = (bf16[2048]{0:T(1024)(128)(2,1)S(1)}, bf16[2048]{0:T(1024)(128)(2,1)}, u32[]{:S(2)}) copy-start(bf16[2048]{0:T(1024)(128)(2,1)} %param.21) | copy-start | bytes 12292
  38.2 2.0 copy-start.2
  42.0 6.2 %copy-start.6 = (bf16[1024,576]{0,1:T(8,128)(2,1)S(1)}, bf16[1024,576]{0,1:T(8,128)(2,1)}, u32[]{:S(2)}) copy-start(bf16[1024,576]{0,1:T(8,128)(2,1)} %get-tuple-element.36) | copy-start | bytes 3538948 | tf_op jit(solution)/shard_map/cond
  49.6 5.2 %copy-start.7 = (f32[1024,1024]{0,1:T(8,128)S(1)}, f32[1024,1024]{0,1:T(8,128)}, u32[]{:S(2)}) copy-start(f32[1024,1024]{0,1:T(8,128)} %get-tuple-element.41) | copy-start | bytes 12582916 | tf_op jit(solution)/shard_map/cond
  56.0 3.5 copy-start.5
  67.0 4.0 copy-start.8
  72.7 3.5 copy-start.4
  76.2 5.9 %copy-start.10 = (s32[768]{0:T(1024)S(1)}, s32[768]{0:T(1024)}, u32[]{:S(2)}) copy-start(s32[768]{0:T(1024)} %get-tuple-element.75) | copy-start | bytes 9220
  106.8 140.9 %all-to-all-start = ((bf16[16,96,2048]{2,1,0:T(8,128)(2,1)}), bf16[16,96,2048]{2,1,0:T(8,128)(2,1)}, u32[]{:S(2)}, u32[]{:S(2)}) async-start(bf16[16,96,2048]{2,1,0:T(8,128)(2,1)} %bitcast.105), calls=%async_computation | async-start | bytes 12582912 | tf_op jit(solution)/shard_map/all_to_all | solution.py:160
  112.2 158.9 %all-gather.8.cloned.1.call-start = ((), (), s32[]{:S(2)}) async-start(), calls=%async_computation.3 | async-start | bytes 7864320 | tf_op jit(solution)/shard_map/all_gather | solution.py:170
  280.7 3.4 copy-start.3
  280.7 7.2 %copy-start.13 = (f32[1,128,6]{1,0,2:T(1,128)S(1)}, f32[1,128,6]{1,0,2:T(1,128)}, u32[]{:S(2)}) copy-start(f32[1,128,6]{1,0,2:T(1,128)} %param.23) | copy-start | bytes 9220
  284.0 9.1 %collective-permute-start = (bf16[2,96,2048]{2,1,0:T(8,128)(2,1)}, bf16[2,96,2048]{2,1,0:T(8,128)(2,1)}, u32[]{:S(2)}, u32[]{:S(2)}) collective-permute-start(bf16[2,96,2048]{2,1,0:T(8,128)(2,1)} %get-tuple-element.50), channel_id=1, source_target_pairs={{0,1},{1,0},{2,3},{3,2},{4,5},{5,4},{6,7},{7,6},{8,9},{9,8},{10,11... | collective-permute-start | bytes 2359304 | tf_op jit(solution)/shard_map/ppermute | solution.py:183
  284.5 51.4 %collective-permute-start.1 = (bf16[2,96,2048]{2,1,0:T(8,128)(2,1)}, bf16[2,96,2048]{2,1,0:T(8,128)(2,1)}, u32[]{:S(2)}, u32[]{:S(2)}) collective-permute-start(bf16[2,96,2048]{2,1,0:T(8,128)(2,1)} %get-tuple-element.49), channel_id=1, source_target_pairs={{0,2},{1,3},{2,0},{3,1},{4,6},{5,7},{6,4},{7,5},{8,10},{9,11},{10,... | collective-permute-start | bytes 2359304 | tf_op jit(solution)/shard_map/ppermute | solution.py:183
  288.0 64.8 %collective-permute-start.2 = (bf16[2,96,2048]{2,1,0:T(8,128)(2,1)}, bf16[2,96,2048]{2,1,0:T(8,128)(2,1)S(1)}, u32[]{:S(2)}, u32[]{:S(2)}) collective-permute-start(bf16[2,96,2048]{2,1,0:T(8,128)(2,1)} %get-tuple-element.48), channel_id=1, source_target_pairs={{0,3},{1,2},{2,1},{3,0},{4,7},{5,6},{6,5},{7,4},{8,11},{9,10},{10,... | collective-permute-start | bytes 2359304 | tf_op jit(solution)/shard_map/ppermute | solution.py:183
  288.1 65.8 %collective-permute-start.3 = (bf16[2,96,2048]{2,1,0:T(8,128)(2,1)S(1)}, bf16[2,96,2048]{2,1,0:T(8,128)(2,1)S(1)}, u32[]{:S(2)}, u32[]{:S(2)}) collective-permute-start(bf16[2,96,2048]{2,1,0:T(8,128)(2,1)S(1)} %get-tuple-element.47), channel_id=1, source_target_pairs={{0,4},{1,5},{2,6},{3,7},{4,0},{5,1},{6,2},{7,3},{8,12},{9,13},{10,... | collective-permute-start | bytes 2359304 | tf_op jit(solution)/shard_map/ppermute | solution.py:183
  289.5 101.1 %collective-permute-start.4 = (bf16[2,96,2048]{2,1,0:T(8,128)(2,1)S(1)}, bf16[2,96,2048]{2,1,0:T(8,128)(2,1)S(1)}, u32[]{:S(2)}, u32[]{:S(2)}) collective-permute-start(bf16[2,96,2048]{2,1,0:T(8,128)(2,1)S(1)} %get-tuple-element.46), channel_id=1, source_target_pairs={{0,5},{1,4},{2,7},{3,6},{4,1},{5,0},{6,3},{7,2},{8,13},{9,12},{10,... | collective-permute-start | bytes 2359304 | tf_op jit(solution)/shard_map/ppermute | solution.py:183
  293.1 116.4 %collective-permute-start.5 = (bf16[2,96,2048]{2,1,0:T(8,128)(2,1)S(1)}, bf16[2,96,2048]{2,1,0:T(8,128)(2,1)S(1)}, u32[]{:S(2)}, u32[]{:S(2)}) collective-permute-start(bf16[2,96,2048]{2,1,0:T(8,128)(2,1)S(1)} %get-tuple-element.45), channel_id=1, source_target_pairs={{0,6},{1,7},{2,4},{3,5},{4,2},{5,3},{6,0},{7,1},{8,14},{9,15},{10,... | collective-permute-start | bytes 2359304 | tf_op jit(solution)/shard_map/ppermute | solution.py:183
  335.9 90.8 %collective-permute-start.6 = (bf16[2,96,2048]{2,1,0:T(8,128)(2,1)S(1)}, bf16[2,96,2048]{2,1,0:T(8,128)(2,1)S(1)}, u32[]{:S(2)}, u32[]{:S(2)}) collective-permute-start(bf16[2,96,2048]{2,1,0:T(8,128)(2,1)S(1)} %get-tuple-element.44), channel_id=1, source_target_pairs={{0,7},{1,6},{2,5},{3,4},{4,3},{5,2},{6,1},{7,0},{8,15},{9,14},{10,... | collective-permute-start | bytes 2359304 | tf_op jit(solution)/shard_map/ppermute | solution.py:183
  451.5 7.6 %copy-start.1 = (bf16[2048,576]{0,1:T(8,128)(2,1)S(1)}, bf16[2048,576]{0,1:T(8,128)(2,1)}, u32[]{:S(2)}) copy-start(bf16[2048,576]{0,1:T(8,128)(2,1)} %param.17) | copy-start | bytes 7077892
Sparse Core Ops, SparseCore 0:
  12.6 27.5 all-gather.3
  42.0 119.6 all-gather.5
  163.6 70.1 all-gather.7
